TPU v7x, 512 devices: a whole 4x8x8 slice. The times are simulated.
512 devices in a mesh: dp: 32 (over z, y_hi), segment: 2 (over y_lo), mp: 8 (over x, core).
Axes of the slice: x: 4, y: 8 (y_hi: 4, y_lo: 2; y = y_hi * 2 + y_lo), z: 8, core: 2. Of those that a mesh axis runs over, the one named last changes fastest.
Arguments:
- prefix_hidden: bfloat16 [64, 512, 8192], P(('dp', 'segment'), 'mp'), may hold values from -16 to 16
- norm_gain: float32 [8192], replicated, may hold values from 0.5 to 1.5
- kv_weight: bfloat16 [8192, 2, 1024], P('dp', None, 'mp'), may hold values from -0.0625 to 0.0625
- action_query: bfloat16 [64, 128, 2048], P(('dp', 'segment'), None, 'mp'), may hold values from -104 to 104
- action_kv: bfloat16 [64, 128, 2, 1024], P(('dp', 'segment'), None, None, 'mp'), may hold values from -4.25 to 4.25
- out_cotangent: bfloat16 [64, 128, 2048], P(('dp', 'segment'), None, 'mp'), may hold values from -18 to 18
- prefix_blocks: int32 [64, 512], P(('dp', 'segment')), may hold values from 0 to 7, as said below
- action_blocks: int32 [64, 128], P(('dp', 'segment')), may hold values from 0 to 8, as said below
- prefix_lengths: int32 [64], P(('dp', 'segment')), may hold values from 128 to 512, as said below
- timesteps: int32 [64], P(('dp', 'segment')), may hold values from 0 to 999
Outputs:
- attn_out: bfloat16 [64, 128, 2048], P(('dp', 'segment'), None, 'mp')
- query_grad: float32 [64, 128, 2048], P(('dp', 'segment'), None, 'mp')
- action_kv_grad: float32 [64, 128, 2, 1024], P(('dp', 'segment'), None, None, 'mp')
- weight_grad: float32 [8192, 2, 1024], P('dp', None, 'mp')
Inputs may be any that keep to these rules, and one draw needn't show every extreme that they name: `prefix_blocks`: constant over each run of 64 positions, 0 on the first run, rising by 0 or 1 from one run to the next; in every draw some sample rises at every run. `action_blocks`: constant over each run of 64 positions; the last run of every sample holds 8; in every draw some sample's first run holds 0. `prefix_lengths`: in every draw some sample's prefix is whole and some sample's is 128.
All inputs are finite; a program needn't handle non-finite values.
Results may differ from a plain program's by a relative error of at most 0.017.
Values may be sent and summed in bfloat16 or wider, within the bound.
No kernel may reach another device: no remote copies, remote signals or barrier semaphores. Data moves between devices by JAX's collectives and lax.ppermute only.
A program may use at most 64 MiB of HBM per device.

v0:
```python
import jax
import jax.numpy as jnp
from jax import lax
from jax.sharding import Mesh
from jax.sharding import PartitionSpec as P

KVH = 8
HD = 128
QH = 16
STEPS = 1000
DP = ("dp_0", "dp_1")
DP_SEGMENT = ("dp_0", "dp_1", "segment")
EPS = 1e-06
NEGATIVE = -1e30


def sum_by_axis(terms, axes):
    subtotal = terms.astype(jnp.bfloat16)
    for axis in axes:
        subtotal = lax.psum_scatter(subtotal, axis, scatter_dimension=0, tiled=True)
    return subtotal.astype(jnp.float32)


def from_everyone(array, axis):
    copies = jnp.broadcast_to(array, (lax.axis_size(axis), *array.shape))
    return lax.all_to_all(copies, axis, split_axis=0, concat_axis=0, tiled=True)


def taken_together(array, axis):
    everything = from_everyone(array, axis)
    return jnp.sum(everything.astype(jnp.float32), axis=0)


def head_scores(query, keys):
    return jnp.einsum("agrh,jgh->graj", query, keys, preferred_element_type=jnp.float32) * HD ** (
        -0.5
    )


def backward_terms(probs, values, keys, query, grad_out):
    probs_low = probs.astype(jnp.bfloat16)
    d_probs = jnp.einsum("agrh,jgh->graj", grad_out, values, preferred_element_type=jnp.float32)
    delta = jnp.sum(probs * d_probs, axis=-1, keepdims=True)
    d_scores = (probs * (d_probs - delta)).astype(jnp.bfloat16)
    d_query = jnp.einsum(
        "graj,jgh->agrh", d_scores, keys, preferred_element_type=jnp.float32
    ) * HD ** (-0.5)
    d_keys = jnp.einsum(
        "graj,agrh->jgh", d_scores, query, preferred_element_type=jnp.float32
    ) * HD ** (-0.5)
    d_values = jnp.einsum("graj,agrh->jgh", probs_low, grad_out, preferred_element_type=jnp.float32)
    return (d_query, jnp.stack([d_keys, d_values], axis=1))


def shards(
    prefix_hidden,
    norm_gain,
    kv_weight,
    action_query,
    action_kv,
    out_cotangent,
    prefix_blocks,
    action_blocks,
    prefix_lengths,
    timesteps,
):
    acts = action_query.shape[1]
    heads_kv = kv_weight.shape[2] // HD
    ratio = QH // KVH
    columns = 2 * kv_weight.shape[2]
    wide = prefix_hidden[0].astype(jnp.float32)
    inverse = lax.rsqrt(jnp.mean(wide * wide, axis=-1, keepdims=True) + EPS)
    normed_local = (wide * inverse * norm_gain).astype(jnp.bfloat16)
    normed = lax.all_gather(normed_local, "mp", axis=0, tiled=True)
    rows = normed.shape[0]
    piece = lax.all_gather(kv_weight, DP, axis=0, tiled=True)
    section = normed
    projected = jnp.dot(
        section, piece.reshape(piece.shape[0], columns), preferred_element_type=jnp.float32
    )
    prefix_kv = projected.astype(jnp.bfloat16).reshape(rows, 2, heads_kv, HD)
    own_pair = action_kv[0].reshape(acts, 2, heads_kv, HD)
    query = action_query[0].reshape(acts, heads_kv, ratio, HD)
    flow_weight = 0.5 + (timesteps[0].astype(jnp.float32) + 0.5) / STEPS
    grad_out = (
        (flow_weight * out_cotangent[0].astype(jnp.float32))
        .astype(jnp.bfloat16)
        .reshape(acts, heads_kv, ratio, HD)
    )
    pblocks = prefix_blocks[0]
    ablocks = action_blocks[0]
    length = prefix_lengths[0]
    keys = jnp.concatenate([prefix_kv[:, 0], own_pair[:, 0]], axis=0)
    values = jnp.concatenate([prefix_kv[:, 1], own_pair[:, 1]], axis=0)
    positions = jnp.arange(rows, dtype=jnp.int32)
    see_prefix = (pblocks[None, :] <= ablocks[:, None]) & (positions[None, :] < length)
    see_action = ablocks[None, :] <= ablocks[:, None]
    visible = jnp.concatenate([see_prefix, see_action], axis=1)
    masked = jnp.where(visible, head_scores(query, keys), NEGATIVE)
    top = jnp.max(masked, axis=-1, keepdims=True)
    expo = jnp.where(visible, jnp.exp(masked - top), 0.0)
    probs = expo / jnp.sum(expo, axis=-1, keepdims=True)
    out = jnp.einsum(
        "graj,jgh->agrh", probs.astype(jnp.bfloat16), values, preferred_element_type=jnp.float32
    )
    d_query, d_pair = backward_terms(probs, values, keys, query, grad_out)
    d_prefix = d_pair[:rows]
    d_action = d_pair[rows:]
    attn_out = out.astype(jnp.bfloat16).reshape(1, acts, ratio * heads_kv * HD)
    query_grad = d_query.reshape(1, acts, ratio * heads_kv * HD)
    action_kv_grad = d_action.reshape(1, acts, 2, heads_kv * HD)
    prefix_grad = d_prefix.astype(jnp.bfloat16).reshape(rows, columns)
    section = normed
    term = lax.dot_general(
        section, prefix_grad, (((0,), (0,)), ((), ())), preferred_element_type=jnp.float32
    )
    shard = sum_by_axis(term.reshape(kv_weight.shape[0] * lax.axis_size(DP), 2, columns // 2), DP)
    weight_grad = taken_together(shard.astype(jnp.bfloat16), "segment").astype(jnp.float32)
    return (attn_out, query_grad, action_kv_grad, weight_grad)


def solution(mesh):
    torus = Mesh(
        mesh.devices.reshape(8, 4, mesh.shape["segment"], mesh.shape["mp"]),
        ("dp_0", "dp_1", "segment", "mp"),
    )
    placed = (
        P(DP_SEGMENT, "mp", None),
        P(),
        P(DP, None, "mp"),
        P(DP_SEGMENT, None, "mp"),
        P(DP_SEGMENT, None, None, "mp"),
        P(DP_SEGMENT, None, "mp"),
        P(DP_SEGMENT, None),
        P(DP_SEGMENT, None),
        P(DP_SEGMENT),
        P(DP_SEGMENT),
    )
    return jax.shard_map(
        shards,
        mesh=torus,
        in_specs=placed,
        out_specs=(
            P(DP_SEGMENT, None, "mp"),
            P(DP_SEGMENT, None, "mp"),
            P(DP_SEGMENT, None, None, "mp"),
            P(DP, None, "mp"),
        ),
        check_vma=False,
    )
```

profile of v0, /device:TPU:18, one launch (start us, length us, event | category | flops | bytes accessed | tf_op | source)
XLA Modules:
  0.0 294.3 jit_solution(14425961718619464857)
XLA Ops:
  7.3 0.7 all-gather.5.cloned.1.call-update
  8.0 1.5 fusion.4
  9.5 2.6 fusion.6
  12.2 0.0 reduce-scatter.3.cloned.1.call-start
  12.2 0.1 copy.52
  12.4 0.1 copy.77
  13.8 0.1 copy.78
  14.0 0.1 broadcast_compare_fusion
  14.1 0.2 compare_and_fusion
  14.3 102.6 %all-gather.5.cloned.1.call-done = bf16[8192,2,128]{2,1,0:T(2,128)(2,1)} async-done(((bf16[256,2,128]{2,1,0:T(2,128)(2,1)}), bf16[8192,2,128]{2,1,0:T(2,128)(2,1)}) %all-gather.5.cloned.1.call-update) | async-done | bytes 4194320 | tf_op jit(solution)/shard_map/all_gather | solution.py:76
  116.9 54.1 %all-gather.3.cloned.1.call-done = bf16[512,8192]{1,0:T(8,128)(2,1)} async-done(((bf16[64,8192]{1,0:T(8,128)(2,1)}), bf16[512,8192]{1,0:T(8,128)(2,1)}) %all-gather.3.cloned.1.call-update) | async-done | bytes 8388624 | tf_op jit(solution)/shard_map/all_gather | solution.py:74
  170.9 6.9 %fusion.8 = bf16[512,256]{0,1:T(8,128)(2,1)S(1)} fusion(bf16[512,8192]{1,0:T(8,128)(2,1)} %all-gather.3.cloned.1.call-done, bf16[1024,8,2,128]{3,2,1,0:T(2,128)(2,1)} %bitcast.129), kind=kOutput, calls=%fused_computation.13 | convolution fusion | flops 2147614720 | bytes 12845056 | tf_op jit(solution)/shard_map/dot_general | solution.py:78
  177.9 0.1 copy.76
  178.0 0.3 fusion.33
  178.3 0.1 fusion.15
  178.5 0.3 convolution_bitcast_fusion.1
  178.8 0.3 multiply_reduce_fusion
  179.1 0.2 fusion.17
  179.3 0.2 fusion.13
  179.6 2.3 copy-done.5
  181.8 4.0 %convolution_convert_fusion = bf16[8192,2,128]{2,0,1:T(8,128)(2,1)} fusion(bf16[512,8192]{1,0:T(8,128)(2,1)S(1)} %copy-done.5, f32[640,1,1,128]{0,3,2,1:T(8,128)S(1)} %convolution_bitcast_fusion.1, f32[640,1,1,128]{0,3,2,1:T(8,128)S(1)} %fusion.13), kind=kOutput, calls=%fused_computation | convolution fusion | flops 2150105088 | bytes 13238272 | tf_op jit(solution)/shard_map/dot_general | solution.py:114
  185.9 59.9 %reduce-scatter.3.cloned.1.call-done = bf16[1024,2,128]{2,0,1:T(8,128)(2,1)} async-done(((bf16[8192,2,128]{2,0,1:T(8,128)(2,1)}), bf16[1024,2,128]{2,0,1:T(8,128)(2,1)}) %reduce-scatter.3.cloned.1.call-update) | async-done | bytes 524304 | tf_op jit(solution)/shard_map/reduce_scatter | solution.py:20
  245.8 0.3 convolution_convert_fusion.1
  246.1 0.7 copy.64
  246.8 29.7 %reduce-scatter.5.cloned.1.call-done = bf16[256,2,128]{2,0,1:T(8,128)(2,1)} async-done(((bf16[1024,2,128]{2,0,1:T(8,128)(2,1)}), bf16[256,2,128]{2,0,1:T(8,128)(2,1)}) %reduce-scatter.5.cloned.1.call-update) | async-done | bytes 131088 | tf_op jit(solution)/shard_map/reduce_scatter | solution.py:20
  276.6 1.6 broadcast_in_dim.24
  278.2 3.4 %all-to-all-start = ((bf16[2,256,2,128]{3,1,2,0:T(8,128)(2,1)}), bf16[2,256,2,128]{3,1,2,0:T(8,128)(2,1)S(1)}, u32[]{:S(2)}, u32[]{:S(2)}) async-start(bf16[2,256,2,128]{3,1,2,0:T(8,128)(2,1)} %broadcast_in_dim.24), calls=%async_computation.2 | async-start | bytes 524288 | tf_op jit(solution)/shard_map/all_to_all | solution.py:26
  281.7 0.3 convolution_multiply_fusion.1
  281.9 0.8 copy.65
  282.7 0.8 copy.66
  283.4 3.4 %all-to-all-done = bf16[2,256,2,128]{3,1,2,0:T(8,128)(2,1)S(1)} async-done(((bf16[2,256,2,128]{3,1,2,0:T(8,128)(2,1)}), bf16[2,256,2,128]{3,1,2,0:T(8,128)(2,1)S(1)}, u32[]{:S(2)}, u32[]{:S(2)}) %all-to-all-start) | async-done | bytes 262176 | tf_op jit(solution)/shard_map/all_to_all | solution.py:26
  286.8 0.9 copy.67
  (27 shorter events, 0.3 us)
Async XLA Ops:
  7.2 5.0 %copy-start = (bf16[1,128,2,128]{3,2,1,0:T(2,128)(2,1)S(1)}, bf16[1,128,2,128]{3,2,1,0:T(2,128)(2,1)}, u32[]{:S(2)}) copy-start(bf16[1,128,2,128]{3,2,1,0:T(2,128)(2,1)} %param.14) | copy-start | bytes 196612
  7.2 5.2 %copy-start.1 = (bf16[1,128,256]{2,1,0:T(8,128)(2,1)S(1)}, bf16[1,128,256]{2,1,0:T(8,128)(2,1)}, u32[]{:S(2)}) copy-start(bf16[1,128,256]{2,1,0:T(8,128)(2,1)} %param.13) | copy-start | bytes 196612
  7.2 6.6 %copy-start.2 = (bf16[1,128,256]{2,1,0:T(8,128)(2,1)S(1)}, bf16[1,128,256]{2,1,0:T(8,128)(2,1)}, u32[]{:S(2)}) copy-start(bf16[1,128,256]{2,1,0:T(8,128)(2,1)} %param.15) | copy-start | bytes 196612
  7.2 6.8 %copy-start.3 = (s32[1,128]{1,0:T(1,128)S(1)}, s32[1,128]{1,0:T(1,128)}, u32[]{:S(2)}) copy-start(s32[1,128]{1,0:T(1,128)} %param.17) | copy-start | bytes 1540
  7.2 6.9 %copy-start.4 = (s32[1,512]{1,0:T(1,128)S(1)}, s32[1,512]{1,0:T(1,128)}, u32[]{:S(2)}) copy-start(s32[1,512]{1,0:T(1,128)} %param.16) | copy-start | bytes 6148
  7.2 109.6 %all-gather.5.cloned.1.call-start = ((), (), s32[]{:S(2)}) async-start(), calls=%async_computation.4 | async-start | bytes 4325376 | tf_op jit(solution)/shard_map/all_gather | solution.py:76
  8.0 163.0 %all-gather.3.cloned.1.call-start = ((), (), s32[]{:S(2)}) async-start(), calls=%async_computation.3 | async-start | bytes 9437184 | tf_op jit(solution)/shard_map/all_gather | solution.py:74
  12.2 233.6 %reduce-scatter.3.cloned.1.call-start = ((), (), s32[]{:S(2)}) async-start(), calls=%async_computation.5 | async-start | bytes 4718592 | tf_op jit(solution)/shard_map/reduce_scatter | solution.py:20
  178.5 3.4 %copy-start.5 = (bf16[512,8192]{1,0:T(8,128)(2,1)S(1)}, bf16[512,8192]{1,0:T(8,128)(2,1)}, u32[]{:S(2)}) copy-start(bf16[512,8192]{1,0:T(8,128)(2,1)} %all-gather.3.cloned.1.call-done) | copy-start | bytes 25165828
  185.8 90.7 %reduce-scatter.5.cloned.1.call-start = ((), (), s32[]{:S(2)}) async-start(), calls=%async_computation.6 | async-start | bytes 655360 | tf_op jit(solution)/shard_map/reduce_scatter | solution.py:20
  278.2 8.6 %all-to-all-start = ((bf16[2,256,2,128]{3,1,2,0:T(8,128)(2,1)}), bf16[2,256,2,128]{3,1,2,0:T(8,128)(2,1)S(1)}, u32[]{:S(2)}, u32[]{:S(2)}) async-start(bf16[2,256,2,128]{3,1,2,0:T(8,128)(2,1)} %broadcast_in_dim.24), calls=%async_computation.2 | async-start | bytes 524288 | tf_op jit(solution)/shard_map/all_to_all | solution.py:26
Sparse Core Ops, SparseCore 0:
  11.2 105.6 all-gather.4
  119.0 51.8 all-gather.2
  185.9 59.7 reduce-scatter.2
  248.4 28.1 reduce-scatter.4
where the time goes:
time: 295 us; the launch traced here: 294 us
  waiting for transfers between devices  250 us (85%)
  between operations  15.3 us (5%)
  matrix products  12.6 us (4%)
  local copies, waits for them, and re-layouts  7.58 us (3%)
  other arithmetic  4.84 us (2%)
  starting transfers between devices  3.6 us (1%)
    all_gather x1, waiting for transfers between devices, shards(): piece = lax.all_gather(kv_weight, DP, axis=0, tiled=True)  103 us
    reduce_scatter x2, waiting for transfers between devices, sum_by_axis(): subtotal = lax.psum_scatter(subtotal, axis, scatter_dimension=0, tiled=True)  89.6 us
    all_gather x1, waiting for transfers between devices, shards(): normed = lax.all_gather(normed_local, 'mp', axis=0, tiled=True)  54.1 us
    dot_general x1, matrix products, shards(): jnp.dot(section, piece.reshape(piece.shape[0], columns), preferred_elemen...  6.94 us
  transfers between devices with their start and end apart: 5, of which 5 were waited for; matrix products, arithmetic and copies ran while one was open for 3% of the time, Pallas kernels for 0%

commit v1 on v0

--- a/solution.py
+++ b/solution.py
@@ -71,7 +71,9 @@
     wide = prefix_hidden[0].astype(jnp.float32)
     inverse = lax.rsqrt(jnp.mean(wide * wide, axis=-1, keepdims=True) + EPS)
     normed_local = (wide * inverse * norm_gain).astype(jnp.bfloat16)
-    normed = lax.all_gather(normed_local, "mp", axis=0, tiled=True)
+    fresh = jnp.stack([normed_local for _ in range(lax.axis_size("mp"))], axis=0)
+    block_last = lax.all_to_all(fresh, "mp", 0, 0)
+    normed = jnp.concatenate(block_last, axis=0)
     rows = normed.shape[0]
     piece = lax.all_gather(kv_weight, DP, axis=0, tiled=True)
     section = normed

time: 295 us -> 244 us (0.83)
  waiting for transfers between devices: 250 us -> 187 us
  matrix products: 12.6 us -> 18.2 us
  starting transfers between devices: 3.6 us -> 9.04 us
    all_gather x1, waiting for transfers between devices: 103 us -> 2.85 us  [shards(): piece = lax.all_gather(kv_weight, DP, axis=0, tiled=True)]
    all_to_all x0 -> x1, waiting for transfers between devices: none -> 91.2 us  [shards(): block_last = lax.all_to_all(fresh, 'mp', 0, 0)]
    all_gather x1 -> x0, waiting for transfers between devices: 54.1 us -> none  [shards(): normed = lax.all_gather(normed_local, 'mp', axis=0, tiled=True)]
    dot_general x1, matrix products: 3.96 us -> 9.58 us  [shards(): lax.dot_general(section, prefix_grad, (((0,), (0,)), ((), ())), preferred...]
    all_to_all x0 -> x1, starting transfers between devices: none -> 5.52 us  [shards(): block_last = lax.all_to_all(fresh, 'mp', 0, 0)]
    another operation x1 -> x2, local copies, waits for them, and re-layouts: 0.11 us -> 4.34 us  [the longest x1 4.23 us: shards(): jnp.stack([normed_local for _ in range(lax.axis_size('mp'))], axis=0)]
  transfers between devices with their start and end apart: 5 -> 5, of which waited for: 5 -> 5; matrix products, arithmetic and copies ran while one was open for 3% -> 4% of each run, Pallas kernels for 0% -> 0%
where the time goes in v1:
time: 244 us; the launch traced here: 243 us
  waiting for transfers between devices  187 us (77%)
  matrix products  18.2 us (7%)
  between operations  15.3 us (6%)
  local copies, waits for them, and re-layouts  9.54 us (4%)
  starting transfers between devices  9.04 us (4%)
  other arithmetic  3.78 us (2%)
    all_to_all x1, waiting for transfers between devices, shards(): block_last = lax.all_to_all(fresh, 'mp', 0, 0)  91.2 us
    reduce_scatter x2, waiting for transfers between devices, sum_by_axis(): subtotal = lax.psum_scatter(subtotal, axis, scatter_dimension=0, tiled=True)  89.4 us
    dot_general x1, matrix products, shards(): lax.dot_general(section, prefix_grad, (((0,), (0,)), ((), ())), preferred...  9.58 us
    dot_general x1, matrix products, shards(): jnp.dot(section, piece.reshape(piece.shape[0], columns), preferred_elemen...  6.94 us
    all_to_all x1, starting transfers between devices, shards(): block_last = lax.all_to_all(fresh, 'mp', 0, 0)  5.52 us
  transfers between devices with their start and end apart: 5, of which 5 were waited for; matrix products, arithmetic and copies ran while one was open for 4% of the time, Pallas kernels for 0%

profile of v1, /device:TPU:18, one launch (start us, length us, event | category | flops | bytes accessed | tf_op | source)
XLA Modules:
  0.0 243.3 jit_solution(14769944003594882466)
XLA Ops:
  7.2 0.7 all-gather.2.cloned.1.call-update
  7.9 1.5 fusion.3
  9.4 1.5 fusion.13
  11.0 4.2 %stack.11 = bf16[8,64,8192]{2,1,0:T(8,128)(2,1)} broadcast(bf16[64,8192]{1,0:T(8,128)(2,1)S(1)} %fusion.13), dimensions={1,2} | broadcast | bytes 9437184 | tf_op jit(solution)/shard_map/stack | solution.py:74
  15.2 5.5 %all-to-all-start = ((bf16[8,64,8192]{2,1,0:T(8,128)(2,1)}), bf16[8,64,8192]{2,1,0:T(8,128)(2,1)}, u32[]{:S(2)}, u32[]{:S(2)}) async-start(bf16[8,64,8192]{2,1,0:T(8,128)(2,1)} %stack.11), calls=%async_computation | async-start | bytes 16777216 | tf_op jit(solution)/shard_map/all_to_all | solution.py:75
  20.8 0.1 copy.73
  20.9 0.1 copy.101
  22.4 0.1 copy.102
  22.5 0.1 broadcast_compare_fusion
  22.6 0.2 compare_and_fusion
  22.8 91.2 %all-to-all-done = bf16[8,64,8192]{2,1,0:T(8,128)(2,1)} async-done(((bf16[8,64,8192]{2,1,0:T(8,128)(2,1)}), bf16[8,64,8192]{2,1,0:T(8,128)(2,1)}, u32[]{:S(2)}, u32[]{:S(2)}) %all-to-all-start) | async-done | bytes 8388640 | tf_op jit(solution)/shard_map/all_to_all | solution.py:75
  114.0 2.8 %all-gather.2.cloned.1.call-done = bf16[8192,2,128]{2,1,0:T(2,128)(2,1)} async-done(((bf16[256,2,128]{2,1,0:T(2,128)(2,1)}), bf16[8192,2,128]{2,1,0:T(2,128)(2,1)}) %all-gather.2.cloned.1.call-update) | async-done | bytes 4194320 | tf_op jit(solution)/shard_map/all_gather | solution.py:78
  116.9 6.9 %fusion.7 = bf16[512,256]{0,1:T(8,128)(2,1)S(1)} fusion(bf16[512,8192]{1,0:T(8,128)(2,1)} %bitcast.1, bf16[1024,8,2,128]{3,2,1,0:T(2,128)(2,1)} %bitcast.128), kind=kOutput, calls=%fused_computation.12 | convolution fusion | flops 2147614720 | bytes 12845056 | tf_op jit(solution)/shard_map/dot_general | solution.py:80
  123.9 0.1 copy.100
  124.0 0.3 fusion.33
  124.3 0.1 fusion.15
  124.4 0.3 convolution_bitcast_fusion.1
  124.7 0.3 multiply_reduce_fusion
  125.1 0.2 fusion.17
  125.3 0.2 fusion.12
  125.5 9.6 %convolution_convert_fusion = bf16[8192,2,128]{2,0,1:T(8,128)(2,1)} fusion(bf16[512,8192,1]{1,0,2:T(8,128)(2,1)} %bitcast.42, f32[640,1,1,128]{0,3,2,1:T(8,128)S(1)} %convolution_bitcast_fusion.1, f32[640,1,1,128]{0,3,2,1:T(8,128)S(1)} %fusion.12), kind=kOutput, calls=%fused_computation | convolution fusion | flops 2150105088 | bytes 13238272 | tf_op jit(solution)/shard_map/dot_general | solution.py:116
  135.2 59.5 %reduce-scatter.3.cloned.1.call-done = bf16[1024,2,128]{2,0,1:T(8,128)(2,1)} async-done(((bf16[8192,2,128]{2,0,1:T(8,128)(2,1)}), bf16[1024,2,128]{2,0,1:T(8,128)(2,1)}) %reduce-scatter.3.cloned.1.call-update) | async-done | bytes 524304 | tf_op jit(solution)/shard_map/reduce_scatter | solution.py:20
  194.7 0.3 convolution_convert_fusion.1
  195.0 0.7 copy.86
  195.7 29.9 %reduce-scatter.5.cloned.1.call-done = bf16[256,2,128]{2,0,1:T(8,128)(2,1)} async-done(((bf16[1024,2,128]{2,0,1:T(8,128)(2,1)}), bf16[256,2,128]{2,0,1:T(8,128)(2,1)}) %reduce-scatter.5.cloned.1.call-update) | async-done | bytes 131088 | tf_op jit(solution)/shard_map/reduce_scatter | solution.py:20
  225.6 1.6 broadcast_in_dim.24
  227.3 3.4 %all-to-all-start.1 = ((bf16[2,256,2,128]{3,1,2,0:T(8,128)(2,1)}), bf16[2,256,2,128]{3,1,2,0:T(8,128)(2,1)S(1)}, u32[]{:S(2)}, u32[]{:S(2)}) async-start(bf16[2,256,2,128]{3,1,2,0:T(8,128)(2,1)} %broadcast_in_dim.24), calls=%async_computation.3 | async-start | bytes 524288 | tf_op jit(solution)/shard_map/all_to_all | solution.py:26
  230.7 0.3 convolution_multiply_fusion.1
  231.0 0.8 copy.87
  231.7 0.8 copy.88
  232.5 3.4 %all-to-all-done.1 = bf16[2,256,2,128]{3,1,2,0:T(8,128)(2,1)S(1)} async-done(((bf16[2,256,2,128]{3,1,2,0:T(8,128)(2,1)}), bf16[2,256,2,128]{3,1,2,0:T(8,128)(2,1)S(1)}, u32[]{:S(2)}, u32[]{:S(2)}) %all-to-all-start.1) | async-done | bytes 262176 | tf_op jit(solution)/shard_map/all_to_all | solution.py:26
  235.9 0.9 copy.89
  (25 shorter events, 0.2 us)
Async XLA Ops:
  7.2 109.7 %all-gather.2.cloned.1.call-start = ((), (), s32[]{:S(2)}) async-start(), calls=%async_computation.4 | async-start | bytes 4325376 | tf_op jit(solution)/shard_map/all_gather | solution.py:78
  15.2 5.5 %copy-start = (bf16[1,128,2,128]{3,2,1,0:T(2,128)(2,1)S(1)}, bf16[1,128,2,128]{3,2,1,0:T(2,128)(2,1)}, u32[]{:S(2)}) copy-start(bf16[1,128,2,128]{3,2,1,0:T(2,128)(2,1)} %param.14) | copy-start | bytes 196612
  15.2 5.7 %copy-start.1 = (bf16[1,128,256]{2,1,0:T(8,128)(2,1)S(1)}, bf16[1,128,256]{2,1,0:T(8,128)(2,1)}, u32[]{:S(2)}) copy-start(bf16[1,128,256]{2,1,0:T(8,128)(2,1)} %param.13) | copy-start | bytes 196612
  15.2 7.1 %copy-start.2 = (bf16[1,128,256]{2,1,0:T(8,128)(2,1)S(1)}, bf16[1,128,256]{2,1,0:T(8,128)(2,1)}, u32[]{:S(2)}) copy-start(bf16[1,128,256]{2,1,0:T(8,128)(2,1)} %param.15) | copy-start | bytes 196612
  15.2 7.3 %copy-start.3 = (s32[1,128]{1,0:T(1,128)S(1)}, s32[1,128]{1,0:T(1,128)}, u32[]{:S(2)}) copy-start(s32[1,128]{1,0:T(1,128)} %param.17) | copy-start | bytes 1540
  15.2 7.4 %copy-start.4 = (s32[1,512]{1,0:T(1,128)S(1)}, s32[1,512]{1,0:T(1,128)}, u32[]{:S(2)}) copy-start(s32[1,512]{1,0:T(1,128)} %param.16) | copy-start | bytes 6148
  15.2 98.8 %all-to-all-start = ((bf16[8,64,8192]{2,1,0:T(8,128)(2,1)}), bf16[8,64,8192]{2,1,0:T(8,128)(2,1)}, u32[]{:S(2)}, u32[]{:S(2)}) async-start(bf16[8,64,8192]{2,1,0:T(8,128)(2,1)} %stack.11), calls=%async_computation | async-start | bytes 16777216 | tf_op jit(solution)/shard_map/all_to_all | solution.py:75
  20.8 173.9 %reduce-scatter.3.cloned.1.call-start = ((), (), s32[]{:S(2)}) async-start(), calls=%async_computation.5 | async-start | bytes 4718592 | tf_op jit(solution)/shard_map/reduce_scatter | solution.py:20
  135.1 90.5 %reduce-scatter.5.cloned.1.call-start = ((), (), s32[]{:S(2)}) async-start(), calls=%async_computation.6 | async-start | bytes 655360 | tf_op jit(solution)/shard_map/reduce_scatter | solution.py:20
  227.3 8.6 %all-to-all-start.1 = ((bf16[2,256,2,128]{3,1,2,0:T(8,128)(2,1)}), bf16[2,256,2,128]{3,1,2,0:T(8,128)(2,1)S(1)}, u32[]{:S(2)}, u32[]{:S(2)}) async-start(bf16[2,256,2,128]{3,1,2,0:T(8,128)(2,1)} %broadcast_in_dim.24), calls=%async_computation.3 | async-start | bytes 524288 | tf_op jit(solution)/shard_map/all_to_all | solution.py:26
Sparse Core Ops, SparseCore 0:
  11.2 105.6 all-gather.1
  135.3 59.3 reduce-scatter.2
  197.5 28.1 reduce-scatter.4
